TPU v7x, 512 devices: a whole 4x4x16 slice. The times are simulated.
512 devices in a mesh: dp: 32 (over y, x, core), mp: 16 (over z).
Axes of the slice: x: 4, y: 4, z: 16, core: 2. Of those that a mesh axis runs over, the one named last changes fastest.
Arguments:
- logged: bfloat16 [8192, 1024], P('dp'), may hold values from -6 to 6
- row_ids: int32 [768], P('dp'), may hold values from 0 to 255
- actions: int32 [768], replicated, may hold values from 0 to 17
- next_actions: int32 [768], replicated, may hold values from 0 to 17
- boot: int32 [16, 768], P('mp'), may hold values from 0 to 767
- dyn_in: bfloat16 [16, 1024, 8192], P('mp', None, 'dp'), may hold values from -0.1875 to 0.1875
- dyn_embed: bfloat16 [16, 18, 8192], P('mp', None, 'dp'), may hold values from -6 to 6
- dyn_out: bfloat16 [16, 8192, 1024], P('mp', 'dp'), may hold values from -0.0625 to 0.0625
- reward_head: bfloat16 [16, 1024], P('mp'), may hold values from -0.1875 to 0.1875
- critic_in: bfloat16 [16, 1024, 4096], P('mp', None, 'dp'), may hold values from -0.1875 to 0.1875
- critic_embed: bfloat16 [16, 18, 4096], P('mp', None, 'dp'), may hold values from -6 to 6
- critic_head: bfloat16 [16, 4096], P('mp', 'dp'), may hold values from -0.09375 to 0.09375
Outputs:
- grad_in: float32 [16, 1024, 4096], P('mp', None, 'dp')
- grad_embed: float32 [16, 18, 4096], P('mp', None, 'dp')
- grad_head: float32 [16, 4096], P('mp', 'dp')
- target: float32 [768], P('dp')
Inputs may be any that keep to these rules, and one draw needn't show every extreme that they name: Row r of the rollout reads logged row (r // 24) * 256 + row_ids[r]. `boot`: indices into all 768 rollout rows, repeats allowed.
All inputs are finite; a program needn't handle non-finite values.
Results may differ from a plain program's by a relative error of at most 0.0029.
Values may be sent and summed in bfloat16 or wider, within the bound.
A program may use at most 64 MiB of HBM per device.

v0:
```python
import jax
import jax.numpy as jnp
from jax import lax
from jax.sharding import PartitionSpec as P

discount = 0.99
penalty_weight = 1.0


def silu_grad(preact):
    sigma_val = jax.nn.sigmoid(preact)
    return sigma_val * (1.0 + preact * (1.0 - sigma_val))


def local(
    logged,
    row_ids,
    actions,
    next_actions,
    boot,
    dyn_in,
    dyn_embed,
    dyn_out,
    reward_head,
    critic_in,
    critic_embed,
    critic_head,
):
    num_actions = dyn_embed.shape[1]
    row_count = row_ids.shape[0]
    my_index = lax.axis_index("dp")
    first_row = my_index * row_count
    picked_rows = jnp.take(logged, row_ids, axis=0)
    states = lax.all_gather(picked_rows, "dp", axis=0, tiled=True)
    act_hot = jax.nn.one_hot(actions, num_actions, dtype=jnp.bfloat16)
    preact = jnp.dot(states, dyn_in[0], preferred_element_type=jnp.float32) + jnp.dot(
        act_hot, dyn_embed[0], preferred_element_type=jnp.float32
    )
    hidden = jax.nn.silu(preact).astype(jnp.bfloat16)
    increment = lax.psum_scatter(
        jnp.dot(hidden, dyn_out[0], preferred_element_type=jnp.float32),
        "dp",
        scatter_dimension=0,
        tiled=True,
    )
    next_state = (picked_rows.astype(jnp.float32) + increment).astype(jnp.bfloat16)
    reward = jnp.dot(next_state, reward_head.T, preferred_element_type=jnp.float32)[:, 0]
    next_local = lax.dynamic_slice_in_dim(next_actions, first_row, row_count, 0)
    next_hot = jax.nn.one_hot(next_local, num_actions, dtype=jnp.bfloat16)
    piece_in = lax.all_gather(critic_in[0], "dp", axis=1, tiled=True)
    piece_embed = lax.all_gather(critic_embed[0], "dp", axis=1, tiled=True)
    piece_head = lax.all_gather(critic_head, "dp", axis=1, tiled=True)
    critic_pre = jnp.dot(next_state, piece_in, preferred_element_type=jnp.float32) + jnp.dot(
        next_hot, piece_embed, preferred_element_type=jnp.float32
    )
    value = jnp.sum(jax.nn.silu(critic_pre) * piece_head.astype(jnp.float32), axis=1)
    bellman = reward + discount * value
    summed, squared = lax.psum((bellman, bellman * bellman), "mp")
    members = lax.axis_size("mp")
    mean_val = summed / members
    spread_val = squared / members - mean_val * mean_val
    target = mean_val - penalty_weight * jnp.sqrt(spread_val + 1.0)
    picks = boot[0]
    boot_states = jnp.take(states, picks, axis=0)
    boot_hot = jnp.take(act_hot, picks, axis=0)
    boot_pre = jnp.dot(boot_states, critic_in[0], preferred_element_type=jnp.float32) + jnp.dot(
        boot_hot, critic_embed[0], preferred_element_type=jnp.float32
    )
    activ = jax.nn.silu(boot_pre)
    head_wide = critic_head.astype(jnp.float32)
    partial_q = jnp.sum(activ * head_wide, axis=1)
    owner_dev = picks // row_count
    target_own = jnp.where(owner_dev == my_index, jnp.take(target, picks % row_count), 0.0)
    q_value, boot_target = lax.psum((partial_q, target_own), "dp")
    residual = q_value - boot_target
    grad_h = jnp.sum(residual[:, None] * activ, axis=0)
    back = (residual[:, None] * head_wide * silu_grad(boot_pre)).astype(jnp.bfloat16)
    grad_w = lax.dot_general(
        boot_states, back, (((0,), (0,)), ((), ())), preferred_element_type=jnp.float32
    )
    grad_e = lax.dot_general(
        boot_hot, back, (((0,), (0,)), ((), ())), preferred_element_type=jnp.float32
    )
    return (grad_w[None], grad_e[None], grad_h[None], target)


def solution(mesh):
    return jax.shard_map(
        local,
        mesh=mesh,
        in_specs=(
            P("dp", None),
            P("dp"),
            P(),
            P(),
            P("mp", None),
            P("mp", None, "dp"),
            P("mp", None, "dp"),
            P("mp", "dp", None),
            P("mp", None),
            P("mp", None, "dp"),
            P("mp", None, "dp"),
            P("mp", "dp"),
        ),
        out_specs=(P("mp", None, "dp"), P("mp", None, "dp"), P("mp", "dp"), P("dp")),
        check_vma=False,
    )
```

profile of v0, /device:TPU:1, one launch (start us, length us, event | category | flops | bytes accessed | tf_op | source)
XLA Modules:
  0.0 388.6 jit_solution(5710124060065360976)
XLA Ops:
  7.2 0.0 copy-start
  7.2 0.0 all-gather.5.cloned.1.call-start
  7.2 0.7 compare_select_fusion.10
  7.9 0.7 compare_and_fusion.1
  8.6 1.8 gather_fusion
  10.4 0.0 copy-start.9
  10.4 0.0 copy-start.12
  10.4 0.7 broadcast_select_fusion.6
  11.1 0.0 all-gather.5.cloned.1.call-update
  11.1 0.0 reduce-scatter.2.cloned.1.call-start
  11.2 64.9 %all-gather.5.cloned.1.call-done = bf16[768,1024]{1,0:T(8,128)(2,1)} async-done(((bf16[24,1024]{1,0:T(8,128)(2,1)}), bf16[768,1024]{1,0:T(8,128)(2,1)}) %all-gather.5.cloned.1.call-update) | async-done | bytes 1572880 | tf_op jit(solution)/shard_map/all_gather | solution.py:34
  76.0 2.1 fusion.6
  78.1 0.0 copy-done
  78.1 0.0 copy-done.9
  78.1 0.0 copy-done.12
  78.2 2.6 fusion.3
  80.8 0.0 copy-start.11
  80.8 0.0 copy-start.7
  80.8 0.0 reduce-scatter.2.cloned.1.call-update
  80.8 0.0 copy-start.8
  80.8 0.0 copy-start.1
  80.8 0.0 all-gather.7.cloned.1.call-start
  80.9 0.7 all-gather.7.cloned.1.call-update
  81.6 0.0 copy-done.11
  81.6 20.5 %all_gather.15 = bf16[1,4096]{1,0:T(2,128)(2,1)S(1)} all-gather(bf16[1,128]{1,0:T(2,128)(2,1)S(1)} %copy-done.11), channel_id=1, replica_groups=mesh['dp'=32,'mp'=16] {'dp'}, dimensions={1}, use_global_device_ids=true | all-gather | bytes 8448 | tf_op jit(solution)/shard_map/all_gather | solution.py:52
  102.1 0.0 copy-done.7
  102.2 0.8 dynamic_slice.3
  103.0 0.2 fusion.10
  103.1 1.9 gather_fusion.2
  105.0 0.0 copy-done.8
  105.0 22.4 %all-gather.1 = bf16[1,18,4096]{2,1,0:T(8,128)(2,1)S(1)} all-gather(bf16[1,18,128]{2,1,0:T(8,128)(2,1)S(1)} %copy-done.8), channel_id=3, replica_groups=mesh['dp'=32,'mp'=16] {'dp'}, dimensions={2}, use_global_device_ids=true | all-gather | bytes 152064 | tf_op jit(solution)/shard_map/all_gather | solution.py:51
  127.5 0.0 copy-done.1
  127.5 0.0 copy-start.6
  127.5 3.6 gather_fusion.1
  131.1 0.0 copy-done.6
  131.1 2.0 fusion.4
  133.1 0.0 copy-start.3
  133.1 0.4 multiply_reduce_fusion.2
  133.5 48.3 %reduce-scatter.2.cloned.1.call-done = f32[24,1024]{1,0:T(8,128)} async-done(((f32[768,1024]{1,0:T(8,128)}), f32[24,1024]{1,0:T(8,128)}) %reduce-scatter.2.cloned.1.call-update) | async-done | bytes 98320 | tf_op jit(solution)/shard_map/reduce_scatter | solution.py:40
  181.8 79.9 %all-gather.7.cloned.1.call-done = bf16[1,1024,4096]{2,1,0:T(8,128)(2,1)} async-done(((bf16[1,1024,128]{2,1,0:T(8,128)(2,1)}), bf16[1,1024,4096]{2,1,0:T(8,128)(2,1)}) %all-gather.7.cloned.1.call-update) | async-done | bytes 8388624 | tf_op jit(solution)/shard_map/all_gather | solution.py:50
  261.7 0.0 copy-done.3
  261.7 4.6 %fusion = f32[24,4096]{1,0:T(8,128)S(1)} fusion(bf16[1,1024,4096]{2,1,0:T(8,128)(2,1)} %all-gather.7.cloned.1.call-done, f32[24,1024]{1,0:T(8,128)} %reduce-scatter.2.cloned.1.call-done, bf16[24,1024]{1,0:T(8,128)(2,1)S(1)} %copy-done.3), kind=kOutput, calls=%fused_computation.3 | convolution fusion | flops 201400320 | bytes 8929280 | tf_op jit(solution)/shard_map/dot_general | solution.py:53
  266.4 0.0 copy-start.4
  266.4 0.0 copy-start.10
  266.4 0.4 multiply_reduce_fusion.1
  266.8 0.5 copy-done.4
  267.3 0.0 copy-done.10
  267.3 0.1 fusion.32
  267.4 24.7 %all-reduce.1 = (f32[24]{0:T(128)S(1)}, f32[24]{0:T(128)S(1)}) all-reduce(f32[24]{0:T(128)S(1)} %get-tuple-element.59, f32[24]{0:T(128)S(1)} %get-tuple-element.60), channel_id=1, replica_groups=mesh['dp'=32,'mp'=16] {'mp'}, use_global_device_ids=true, to_apply=%region_5.6 | all-reduce | flops 48 | bytes 384 | tf_op jit(solution)/shard_map/psum | solution.py:58
  292.1 0.0 copy-start.5
  292.2 0.7 fusion.30
  292.9 0.0 copy-start.2
  292.9 0.7 fusion.31
  293.6 4.4 %fusion.23 = (f32[768]{0:T(1024)S(1)}, s32[768,1]{0,1:T(1,128)S(1)}) fusion(f32[]{:T(128)} %bitcast.28, f32[]{:T(128)} %bitcast.29, f32[]{:T(128)} %bitcast.30, f32[]{:T(128)} %bitcast.31, f32[]{:T(128)} %bitcast.32, f32[]{:T(128)} %bitcast.34, f32[]{:T(128)} %bitcast.33, s32[1,768]{1,0:T(1,128)S(1)} %copy-done.7), kind=kLoop, calls=%fused_computation.78 | loop fusion | flops 16128 | bytes 9244 | tf_op jit(solution)/shard_map/jit(_take)/gather | solution.py:73
  298.0 0.2 compare_reduce_fusion.16
  298.1 10.7 %fusion.21 = f32[768]{0:T(1024)S(1)} fusion(pred[768]{0:T(1024)(128)(4,1)S(1)} %get-tuple-element.28, pred[768]{0:T(1024)(128)(4,1)S(1)} %get-tuple-element.27, pred[768]{0:T(1024)(128)(4,1)S(1)} %get-tuple-element.26, pred[768]{0:T(1024)(128)(4,1)S(1)} %get-tuple-element.25, pred[768]{0:T(1024)(128)(4,1)S(1)} %get-tuple-element.24, ...), kind=kLoop, calls=%fused_computation.73 | loop fusion | flops 29184 | bytes 22344 | tf_op jit(solution)/shard_map/jit(_where)/select_n | solution.py:73
  308.8 69.8 %all-reduce = (f32[768]{0:T(1024)S(1)}, f32[768]{0:T(1024)S(1)}) all-reduce(f32[768]{0:T(1024)S(1)} %get-tuple-element.61, f32[768]{0:T(1024)S(1)} %fusion.21), channel_id=1, replica_groups=mesh['dp'=32,'mp'=16] {'dp'}, use_global_device_ids=true, to_apply=%region_1.2 | all-reduce | flops 1536 | bytes 12288 | tf_op jit(solution)/shard_map/psum | solution.py:74
  378.7 0.7 multiply_reduce_fusion
  379.4 0.4 convolution_bitcast_fusion.1
  379.8 0.0 copy-done.5
  379.8 0.0 copy-done.2
  379.8 1.7 convolution_bitcast_fusion
  381.5 0.6 copy.17
  (9 shorter events, 0.1 us)
Async XLA Ops:
  7.2 71.0 %copy-start = (bf16[1,256,1024]{2,1,0:T(8,128)(2,1)S(1)}, bf16[1,256,1024]{2,1,0:T(8,128)(2,1)}, u32[]{:S(2)}) copy-start(bf16[1,256,1024]{2,1,0:T(8,128)(2,1)} %param.19) | copy-start | bytes 1572868
  7.2 68.8 %all-gather.5.cloned.1.call-start = ((), (), s32[]{:S(2)}) async-start(), calls=%async_computation.1 | async-start | bytes 1622016 | tf_op jit(solution)/shard_map/all_gather | solution.py:34
  10.4 67.8 %copy-start.9 = (s32[768]{0:T(1024)S(1)}, s32[768]{0:T(1024)}, u32[]{:S(2)}) copy-start(s32[768]{0:T(1024)} %param.14) | copy-start | bytes 9220
  10.4 67.8 %copy-start.12 = (bf16[1,18,256]{2,1,0:T(8,128)(2,1)S(1)}, bf16[1,18,256]{2,1,0:T(8,128)(2,1)}, u32[]{:S(2)}) copy-start(bf16[1,18,256]{2,1,0:T(8,128)(2,1)} %param.18) | copy-start | bytes 27652
  11.1 170.7 %reduce-scatter.2.cloned.1.call-start = ((), (), s32[]{:S(2)}) async-start(), calls=%async_computation.2 | async-start | bytes 3244032 | tf_op jit(solution)/shard_map/reduce_scatter | solution.py:40
  80.8 0.8 copy-start.11
  80.8 21.4 %copy-start.7 = (s32[1,768]{1,0:T(1,128)S(1)}, s32[1,768]{1,0:T(1,128)}, u32[]{:S(2)}) copy-start(s32[1,768]{1,0:T(1,128)} %param.16) | copy-start | bytes 9220
  80.8 24.2 %copy-start.8 = (bf16[1,18,128]{2,1,0:T(8,128)(2,1)S(1)}, bf16[1,18,128]{2,1,0:T(8,128)(2,1)}, u32[]{:S(2)}) copy-start(bf16[1,18,128]{2,1,0:T(8,128)(2,1)} %param.22) | copy-start | bytes 13828
  80.8 46.7 %copy-start.1 = (bf16[768,1024]{1,0:T(8,128)(2,1)S(1)}, bf16[768,1024]{1,0:T(8,128)(2,1)}, u32[]{:S(2)}) copy-start(bf16[768,1024]{1,0:T(8,128)(2,1)} %all-gather.5.cloned.1.call-done) | copy-start | bytes 4718596
  80.8 180.9 %all-gather.7.cloned.1.call-start = ((), (), s32[]{:S(2)}) async-start(), calls=%async_computation.3 | async-start | bytes 8650752 | tf_op jit(solution)/shard_map/all_gather | solution.py:50
  127.5 3.6 copy-start.6
  133.1 128.6 %copy-start.3 = (bf16[24,1024]{1,0:T(8,128)(2,1)S(1)}, bf16[24,1024]{1,0:T(8,128)(2,1)}, u32[]{:S(2)}) copy-start(bf16[24,1024]{1,0:T(8,128)(2,1)} %broadcast_select_fusion.6) | copy-start | bytes 147460
  266.4 0.9 copy-start.4
  266.4 0.9 copy-start.10
  292.1 87.6 %copy-start.5 = (f32[24]{0:T(128)}, f32[24]{0:T(128)S(1)}, u32[]{:S(2)}) copy-start(f32[24]{0:T(128)S(1)} %sqrt_subtract_fusion) | copy-start | bytes 292
  292.9 86.9 %copy-start.2 = (bf16[768,1024]{1,0:T(8,128)(2,1)S(1)}, bf16[768,1024]{1,0:T(8,128)(2,1)}, u32[]{:S(2)}) copy-start(bf16[768,1024]{1,0:T(8,128)(2,1)} %gather_fusion.1) | copy-start | bytes 4718596
Sparse Core Ops, SparseCore 0:
  11.7 64.2 all-gather.4
  80.9 100.8 reduce-scatter.1
  185.3 76.3 all-gather.6
where the time goes:
time: 389 us
  waiting for transfers between devices  194 us (50%)
  blocking collectives  137 us (35%)
  other arithmetic  18.3 us (5%)
  matrix products  14.5 us (4%)
  between operations  14 us (4%)
  local copies, waits for them, and re-layouts  10.5 us (3%)
    all_gather x1, waiting for transfers between devices, local(): piece_in = lax.all_gather(critic_in[0], 'dp', axis=1, tiled=True)  79.9 us
    psum x1, blocking collectives, local(): q_value, boot_target = lax.psum((partial_q, target_own), 'dp')  69.8 us
    all_gather x1, waiting for transfers between devices, local(): states = lax.all_gather(picked_rows, 'dp', axis=0, tiled=True)  64.9 us
    reduce_scatter x1, waiting for transfers between devices, local(): lax.psum_scatter(jnp.dot(hidden, dyn_out[0], preferred_element_type=jnp.f...  48.3 us
    psum x1, blocking collectives, local(): summed, squared = lax.psum((bellman, bellman * bellman), 'mp')  24.7 us
    all_gather x1, blocking collectives, local(): piece_embed = lax.all_gather(critic_embed[0], 'dp', axis=1, tiled=True)  22.4 us
    all_gather x1, blocking collectives, local(): piece_head = lax.all_gather(critic_head, 'dp', axis=1, tiled=True)  20.5 us
    select_n x1, other arithmetic, local(): jnp.where(owner_dev == my_index, jnp.take(target, picks % row_count), 0.0)  10.7 us
  transfers between devices with their start and end apart: 3, of which 3 were waited for; matrix products, arithmetic and copies ran while one was open for 2% of the time, Pallas kernels for 0%

commit v1 on v0

v1 whole, which is shorter than its diff:
```python
import jax
import jax.numpy as jnp
from jax import lax
from jax.experimental import pallas as pl
from jax.experimental.pallas import tpu as pltpu
from jax.sharding import PartitionSpec as P

MESH = pl.DeviceIdType.MESH
F32 = jnp.float32
BF16 = jnp.bfloat16

discount = 0.99
penalty_weight = 1.0

CHUNKS = 3
CHIPS = 16
SIDE = 4
MEMBERS = 16
WIDTH = 1024
HALF = 512
LANES = 128
ACTS = 32


def nt(lhs, rhs):
    return lax.dot_general(lhs, rhs, (((1,), (1,)), ((), ())), preferred_element_type=F32)


def tn(lhs, rhs):
    return lax.dot_general(lhs, rhs, (((0,), (0,)), ((), ())), preferred_element_type=F32)


def nn(lhs, rhs):
    return jnp.dot(lhs, rhs, preferred_element_type=F32)


def sigmoid(v):
    return 0.5 * jnp.tanh(0.5 * v) + 0.5


def fold(block):
    return jnp.concatenate([block[:, :HALF], block[:, HALF:]], axis=0)


def unfold(block):
    return jnp.concatenate([block[:8], block[8:]], axis=1)


def iota(shape, dim):
    return lax.broadcasted_iota(jnp.int32, shape, dim)


def kernel(
    rowid_ref,
    act_ref,
    nact_ref,
    boot_ref,
    rhead_ref,
    chead_ref,
    demb_ref,
    cemb_ref,
    logged_hbm,
    din_hbm,
    dout_hbm,
    cin_hbm,
    gin_ref,
    gemb_ref,
    ghead_ref,
    tgt_ref,
    logv,
    wi,
    wo,
    wc,
    em,
    ce,
    hd,
    ag1,
    xs,
    ep,
    rss,
    rsr,
    ag2,
    wct,
    ecn,
    ecb,
    at,
    gt,
    xt,
    bt,
    acts,
    cnt,
    qv,
    ph6,
    zb,
    fin,
    loc_sem,
    wsend,
    wrecv,
    a_send,
    a_recv,
    r_send,
    r_recv,
    n_send,
    n_recv,
    x_send,
    x_recv,
    s_send,
    s_recv,
):
    dp = lax.axis_index("dp")
    zi = lax.axis_index("mp")
    core = dp % 2
    me = dp // 2
    px = me % SIDE
    py = me // SIDE
    sib = (dp + 1 - 2 * core, zi)

    def peer(step):
        chip = ((py + step // SIDE) % SIDE) * SIDE + (px + step % SIDE) % SIDE
        return chip, (chip * 2 + core, zi)

    loads = [
        pltpu.make_async_copy(logged_hbm, logv, loc_sem.at[0]),
        pltpu.make_async_copy(din_hbm, wi.at[0], loc_sem.at[1]),
        pltpu.make_async_copy(dout_hbm, wo.at[0], loc_sem.at[2]),
        pltpu.make_async_copy(cin_hbm, wc.at[0], loc_sem.at[3]),
    ]
    for load in loads:
        load.start()

    barrier = pltpu.get_barrier_semaphore()

    def greet_z(step, carry):
        pl.semaphore_signal(barrier, inc=1, device_id=(dp, (zi + step) % MEMBERS), device_id_type=MESH)
        return carry

    lax.fori_loop(1, MEMBERS, greet_z, 0)

    def greet(step, carry):
        pl.semaphore_signal(barrier, inc=1, device_id=peer(step)[1], device_id_type=MESH)
        return carry

    lax.fori_loop(1, CHIPS, greet, 0)
    pl.semaphore_signal(barrier, inc=1, device_id=sib, device_id_type=MESH)

    em[0] = nn((iota((ACTS, 18), 0) == iota((ACTS, 18), 1)).astype(BF16), demb_ref[...]).astype(BF16)
    ce[0] = nn((iota((ACTS, 18), 0) == iota((ACTS, 18), 1)).astype(BF16), cemb_ref[...]).astype(BF16)
    hd[0] = jnp.broadcast_to(chead_ref[...].astype(F32), (8, LANES))
    loads[0].wait()
    hot = (iota((256, 24), 0) == rowid_ref[...]).astype(BF16)
    picked = tn(hot, logv[...])
    for ch in range(CHUNKS):
        ag1[ch, me] = fold(picked[ch * 8 : ch * 8 + 8]).astype(BF16)

    pl.semaphore_wait(barrier, 2 * (CHIPS - 1) + 1)

    for ch in range(CHUNKS):

        def send_states(step, carry, ch=ch):
            pltpu.make_async_remote_copy(
                src_ref=ag1.at[ch, me],
                dst_ref=ag1.at[ch, me],
                send_sem=a_send.at[ch],
                recv_sem=a_recv.at[ch],
                device_id=peer(step)[1],
                device_id_type=MESH,
            ).start()
            return carry

        lax.fori_loop(1, CHIPS, send_states, 0)

    swaps = []
    for i, (src, dst) in enumerate(
        [
            (din_hbm, wi.at[1]),
            (em.at[0], em.at[1]),
            (dout_hbm, wo.at[1]),
            (cin_hbm, wc.at[1]),
            (ce.at[0], ce.at[1]),
            (hd.at[0], hd.at[1]),
        ]
    ):
        swaps.append(
            pltpu.make_async_remote_copy(
                src_ref=src,
                dst_ref=dst,
                send_sem=wsend.at[i],
                recv_sem=wrecv.at[i],
                device_id=sib,
                device_id_type=MESH,
            )
        )
        swaps[-1].start()

    lane = iota((1, LANES), 1)
    base = 48 * (lane // 8) + lane % 8
    stacked = jnp.concatenate(
        [act_ref[...].astype(F32), nact_ref[...].astype(F32), jnp.zeros((6, 768), F32)], axis=0
    ).astype(BF16)
    for half in range(2):
        who = core if half == 0 else 1 - core
        for ch in range(CHUNKS):
            rows = base + 24 * who + 8 * ch
            pick = (iota((768, LANES), 0) == rows).astype(BF16)
            acts[half * CHUNKS + ch] = nn(stacked, pick)
            total = jnp.zeros((LANES, LANES), F32)
            for part in range(6):
                column = jnp.broadcast_to(
                    boot_ref[:, part * LANES : (part + 1) * LANES].astype(F32), (LANES, LANES)
                ).T
                total = total + (column == rows.astype(F32)).astype(F32)
            cnt[half * CHUNKS + ch] = jnp.broadcast_to(jnp.sum(total, axis=0, keepdims=True), (8, LANES))

    def hot_t(slot, row):
        return (iota((ACTS, LANES), 0).astype(F32) == acts[slot][row : row + 1]).astype(BF16)

    for load in loads[1:]:
        load.wait()
    swaps[0].wait_recv()
    swaps[1].wait_recv()
    for ch in range(CHUNKS):
        hot_rows = hot_t(ch, 0)
        for s in range(2):
            ep[ch, s] = tn(hot_rows, em[s])
    swaps[2].wait_recv()

    def dynamics(ch, carry):
        slots = ag1.at[ch, pl.ds(0, CHIPS - 1)]
        pltpu.make_async_copy(slots, slots, a_recv.at[ch]).wait()
        x = jnp.concatenate([unfold(ag1[ch, j].astype(F32)) for j in range(CHIPS)], axis=0).astype(BF16)
        xs[0, ch] = x
        pltpu.make_async_remote_copy(
            src_ref=xs.at[0, ch],
            dst_ref=xs.at[1, ch],
            send_sem=x_send.at[ch],
            recv_sem=x_recv.at[ch],
            device_id=sib,
            device_id_type=MESH,
        ).start()
        inc = jnp.zeros((LANES, WIDTH), F32)
        for s in range(2):
            pre = nn(x, wi[s]) + ep[ch, s]
            inc = inc + nn((pre * sigmoid(pre)).astype(BF16), wo[s])
        for j in range(CHIPS):
            rss[ch, j] = fold(inc[j * 8 : j * 8 + 8]).astype(BF16)
        rsr[ch, me] = rss[ch, me]

        def send_sums(step, carry):
            chip, where = peer(step)
            pltpu.make_async_remote_copy(
                src_ref=rss.at[ch, chip],
                dst_ref=rsr.at[ch, me],
                send_sem=r_send.at[ch],
                recv_sem=r_recv.at[ch],
                device_id=where,
                device_id_type=MESH,
            ).start()
            return carry

        lax.fori_loop(1, CHIPS, send_sums, 0)
        return carry

    lax.fori_loop(0, CHUNKS, dynamics, 0)

    for i in range(3, 6):
        swaps[i].wait_recv()
    for s in range(2):
        wct[s * LANES : (s + 1) * LANES] = wc[s].T
    wct[256:272] = jnp.concatenate([rhead_ref[...].astype(F32), jnp.zeros((15, WIDTH), F32)], axis=0).astype(BF16)
    heads = [jnp.broadcast_to(hd[s][:1], (LANES, LANES)).T for s in range(2)]
    for ch in range(CHUNKS):
        for s in range(2):
            ecn[ch, s] = tn(ce[s], hot_t(ch, 1))
            ecb[ch, s] = tn(ce[s], hot_t(ch, 0))
        ecb[CHUNKS + ch, 0] = tn(ce[0], hot_t(CHUNKS + ch, 0))

    def own_units(slot, pre):
        gate = sigmoid(pre)
        act = pre * gate
        at[slot] = act
        gt[slot] = heads[0] * (gate * (1.0 + pre * (1.0 - gate)))
        return act

    for ch in range(CHUNKS):
        x = xs[0, ch]
        pre = nt(wct[:256], x)
        act0 = own_units(ch, pre[:LANES] + ecb[ch, 0])
        pre1 = pre[LANES:] + ecb[ch, 1]
        weighted = act0 * heads[0] + pre1 * sigmoid(pre1) * heads[1]
        qv[ch : ch + 1] = jnp.sum(weighted, axis=0, keepdims=True)
        xt[:, ch * LANES : (ch + 1) * LANES] = x.T

    def finish_rows(ch, carry):
        slots = rsr.at[ch, pl.ds(0, CHIPS - 1)]
        pltpu.make_async_copy(slots, slots, r_recv.at[ch]).wait()
        total = rsr[ch, 0].astype(F32)
        for j in range(1, CHIPS):
            total = total + rsr[ch, j].astype(F32)
        ag2[ch, me] = (ag1[ch, me].astype(F32) + total).astype(BF16)

        def send_next(step, carry):
            pltpu.make_async_remote_copy(
                src_ref=ag2.at[ch, me],
                dst_ref=ag2.at[ch, me],
                send_sem=n_send.at[ch],
                recv_sem=n_recv.at[ch],
                device_id=peer(step)[1],
                device_id_type=MESH,
            ).start()
            return carry

        lax.fori_loop(1, CHIPS, send_next, 0)
        return carry

    lax.fori_loop(0, CHUNKS, finish_rows, 0)

    for ch in range(CHUNKS):
        pltpu.make_async_copy(xs.at[1, ch], xs.at[1, ch], x_recv.at[ch]).wait()
        x = xs[1, ch]
        own_units(CHUNKS + ch, nt(wct[:LANES], x) + ecb[CHUNKS + ch, 0])
        xt[:, (CHUNKS + ch) * LANES : (CHUNKS + ch + 1) * LANES] = x.T

    rewards = []
    for ch in range(CHUNKS):
        slots = ag2.at[ch, pl.ds(0, CHIPS - 1)]
        pltpu.make_async_copy(slots, slots, n_recv.at[ch]).wait()
        x = jnp.concatenate([unfold(ag2[ch, j].astype(F32)) for j in range(CHIPS)], axis=0).astype(BF16)
        pre = nt(wct[...], x)
        pre0 = pre[:LANES] + ecn[ch, 0]
        pre1 = pre[LANES:256] + ecn[ch, 1]
        weighted = pre0 * sigmoid(pre0) * heads[0] + pre1 * sigmoid(pre1) * heads[1]
        ph6[me, ch : ch + 1] = jnp.sum(weighted, axis=0, keepdims=True)
        rewards.append(pre[256:257])
    ph6[me, 3:6] = qv[0:3]
    ph6[me, 6:8] = jnp.zeros((2, LANES), F32)

    far = [t ^ 10 for t in range(CHIPS) if t != 10]
    for step in far:
        pltpu.make_async_remote_copy(
            src_ref=ph6.at[me],
            dst_ref=ph6.at[me],
            send_sem=s_send.at[0],
            recv_sem=s_recv.at[0],
            device_id=peer(step)[1],
            device_id_type=MESH,
        ).start()
    slots = ph6.at[pl.ds(0, CHIPS - 1)]
    pltpu.make_async_copy(slots, slots, s_recv.at[0]).wait()
    sums = ph6[0]
    for j in range(1, CHIPS):
        sums = sums + ph6[j]
    reward = jnp.concatenate(rewards + [jnp.zeros((5, LANES), F32)], axis=0)
    zb[zi] = reward + discount * sums
    for step in (8, 7, 9, 6, 10, 5, 11, 4, 12, 3, 13, 2, 14, 1, 15):
        pltpu.make_async_remote_copy(
            src_ref=zb.at[zi],
            dst_ref=zb.at[zi],
            send_sem=s_send.at[1],
            recv_sem=s_recv.at[1],
            device_id=(dp, (zi + step) % MEMBERS),
            device_id_type=MESH,
        ).start()
    slots = zb.at[pl.ds(0, MEMBERS - 1)]
    pltpu.make_async_copy(slots, slots, s_recv.at[1]).wait()
    total = zb[0]
    square = total * total
    for m in range(1, MEMBERS):
        one = zb[m]
        total = total + one
        square = square + one * one
    mean = total / MEMBERS
    spread = square / MEMBERS - mean * mean
    target = mean - penalty_weight * jnp.sqrt(spread + 1.0)
    fin[0] = jnp.concatenate([target[:3], sums[3:6], jnp.zeros((2, LANES), F32)], axis=0)
    last = pltpu.make_async_remote_copy(
        src_ref=fin.at[0],
        dst_ref=fin.at[1],
        send_sem=s_send.at[2],
        recv_sem=s_recv.at[2],
        device_id=sib,
        device_id_type=MESH,
    )
    last.start()

    turned = pltpu.roll(target, (LANES - 8 * me) % LANES, 1)
    line = turned[0:1]
    for ch in range(1, CHUNKS):
        line = jnp.where(lane // 8 == ch, pltpu.roll(turned, 8 * ch, 1)[ch : ch + 1], line)
    tgt_ref[...] = line[:, :24]

    head_sum = jnp.zeros((LANES, LANES), F32)
    for half in range(2):
        if half == 1:
            last.wait_recv()
        ends = fin[half]
        for ch in range(CHUNKS):
            slot = half * CHUNKS + ch
            scaled = cnt[slot][:1] * (ends[3 + ch : 4 + ch] - ends[ch : ch + 1])
            head_sum = head_sum + scaled * at[slot]
            bt[:, slot * LANES : (slot + 1) * LANES] = (scaled * gt[slot]).astype(BF16)
    back = bt[...]
    gin_ref[...] = nt(xt[...], back)
    hots = jnp.concatenate([hot_t(slot, 0) for slot in range(2 * CHUNKS)], axis=1)
    gemb_ref[...] = nt(hots, back)[:18]
    ghead_ref[...] = jnp.sum(head_sum.T, axis=0, keepdims=True)

    last.wait_send()
    for swap in swaps:
        swap.wait_send()

    def drain(ch, carry):
        for buf, sem in ((ag1, a_send), (rss, r_send), (ag2, n_send)):
            slots = buf.at[ch, pl.ds(0, CHIPS - 1)]
            pltpu.make_async_copy(slots, slots, sem.at[ch]).wait()
        pltpu.make_async_copy(xs.at[0, ch], xs.at[0, ch], x_send.at[ch]).wait()
        return carry

    lax.fori_loop(0, CHUNKS, drain, 0)
    for i, buf in enumerate((ph6, zb)):
        slots = buf.at[pl.ds(0, CHIPS - 1)]
        pltpu.make_async_copy(slots, slots, s_send.at[i]).wait()


def local(
    logged,
    row_ids,
    actions,
    next_actions,
    boot,
    dyn_in,
    dyn_embed,
    dyn_out,
    reward_head,
    critic_in,
    critic_embed,
    critic_head,
):
    vmem = pl.BlockSpec(memory_space=pltpu.VMEM)
    hbm = pl.BlockSpec(memory_space=pl.ANY)
    dma = pltpu.SemaphoreType.DMA
    blocks = (CHUNKS, CHIPS, 16, HALF)
    grad_in, grad_embed, grad_head, target = pl.pallas_call(
        kernel,
        out_shape=(
            jax.ShapeDtypeStruct((WIDTH, LANES), F32),
            jax.ShapeDtypeStruct((18, LANES), F32),
            jax.ShapeDtypeStruct((1, LANES), F32),
            jax.ShapeDtypeStruct((1, 24), F32),
        ),
        in_specs=[vmem] * 8 + [hbm] * 4,
        out_specs=(vmem,) * 4,
        scratch_shapes=[
            pltpu.VMEM((256, WIDTH), BF16),
            pltpu.VMEM((2, WIDTH, 256), BF16),
            pltpu.VMEM((2, 256, WIDTH), BF16),
            pltpu.VMEM((2, WIDTH, LANES), BF16),
            pltpu.VMEM((2, ACTS, 256), BF16),
            pltpu.VMEM((2, ACTS, LANES), BF16),
            pltpu.VMEM((2, 8, LANES), F32),
            pltpu.VMEM(blocks, BF16),
            pltpu.VMEM((2, CHUNKS, LANES, WIDTH), BF16),
            pltpu.VMEM((CHUNKS, 2, LANES, 256), F32),
            pltpu.VMEM(blocks, BF16),
            pltpu.VMEM(blocks, BF16),
            pltpu.VMEM(blocks, BF16),
            pltpu.VMEM((272, WIDTH), BF16),
            pltpu.VMEM((CHUNKS, 2, LANES, LANES), F32),
            pltpu.VMEM((2 * CHUNKS, 2, LANES, LANES), F32),
            pltpu.VMEM((2 * CHUNKS, LANES, LANES), F32),
            pltpu.VMEM((2 * CHUNKS, LANES, LANES), F32),
            pltpu.VMEM((WIDTH, 768), BF16),
            pltpu.VMEM((LANES, 768), BF16),
            pltpu.VMEM((2 * CHUNKS, 8, LANES), F32),
            pltpu.VMEM((2 * CHUNKS, 8, LANES), F32),
            pltpu.VMEM((8, LANES), F32),
            pltpu.VMEM((CHIPS, 8, LANES), F32),
            pltpu.VMEM((MEMBERS, 8, LANES), F32),
            pltpu.VMEM((2, 8, LANES), F32),
            dma((4,)),
            dma((6,)),
            dma((6,)),
            dma((CHUNKS,)),
            dma((CHUNKS,)),
            dma((CHUNKS,)),
            dma((CHUNKS,)),
            dma((CHUNKS,)),
            dma((CHUNKS,)),
            dma((CHUNKS,)),
            dma((CHUNKS,)),
            dma((3,)),
            dma((3,)),
        ],
        compiler_params=pltpu.CompilerParams(
            collective_id=0, has_side_effects=True, vmem_limit_bytes=48 * 2**20
        ),
        name="rollout",
    )(
        row_ids[None],
        actions[None],
        next_actions[None],
        boot,
        reward_head,
        critic_head,
        dyn_embed[0],
        critic_embed[0],
        logged,
        dyn_in[0],
        dyn_out[0],
        critic_in[0],
    )
    return grad_in[None], grad_embed[None], grad_head, target[0]


def solution(mesh):
    return jax.shard_map(
        local,
        mesh=mesh,
        in_specs=(
            P("dp", None),
            P("dp"),
            P(),
            P(),
            P("mp", None),
            P("mp", None, "dp"),
            P("mp", None, "dp"),
            P("mp", "dp", None),
            P("mp", None),
            P("mp", None, "dp"),
            P("mp", None, "dp"),
            P("mp", "dp"),
        ),
        out_specs=(P("mp", None, "dp"), P("mp", None, "dp"), P("mp", "dp"), P("dp")),
        check_vma=False,
    )
```

time: 389 us -> 69.7 us (0.18)
  waiting for transfers between devices: 194 us -> 0 us
  blocking collectives: 137 us -> 0 us
  Pallas kernels: 0 us -> 59.4 us
  other arithmetic: 18.3 us -> 0 us
  matrix products: 14.5 us -> 0 us
  between operations: 14 us -> 0.69 us
    all_gather x2 -> x0, waiting for transfers between devices: 145 us -> none  [the longest x1 79.9 us: local(): piece_in = lax.all_gather(critic_in[0], 'dp', axis=1, tiled=True)]
    psum x2 -> x0, blocking collectives: 94.5 us -> none  [the longest x1 69.8 us: local(): q_value, boot_target = lax.psum((partial_q, target_own), 'dp')]
    pallas_call x0 -> x1, Pallas kernels: none -> 59.4 us  [local(): pl.pallas_call(kernel, out_shape=(jax.ShapeDtypeStruct((WIDTH, LANES), F3...]
    reduce_scatter x1 -> x0, waiting for transfers between devices: 48.3 us -> none  [local(): lax.psum_scatter(jnp.dot(hidden, dyn_out[0], preferred_element_type=jnp.f...]
    all_gather x2 -> x0, blocking collectives: 43 us -> none  [the longest x1 22.4 us: local(): piece_embed = lax.all_gather(critic_embed[0], 'dp', axis=1, tiled=True)]
    dot_general x9 -> x0, matrix products: 14.5 us -> none  [the longest x1 4.64 us: local(): jnp.dot(next_state, piece_in, preferred_element_type=jnp.float32)]
    select_n x4 -> x0, other arithmetic: 12.1 us -> none  [the longest x1 10.7 us: local(): jnp.where(owner_dev == my_index, jnp.take(target, picks % row_count), 0.0)]
    gather x5 -> x0, local copies, waits for them, and re-layouts: 8.62 us -> none  [the longest x1 3.59 us: local(): boot_states = jnp.take(states, picks, axis=0)]
  transfers between devices with their start and end apart: 3 -> 0, of which waited for: 3 -> 0; matrix products, arithmetic and copies ran while one was open for 2% -> 0% of each run, Pallas kernels for 0% -> 0%
where the time goes in v1:
time: 69.7 us; the launch traced here: 69.3 us
  Pallas kernels  59.4 us (85%)
  local copies, waits for them, and re-layouts  9.23 us (13%)
    pallas_call x1, Pallas kernels, local(): pl.pallas_call(kernel, out_shape=(jax.ShapeDtypeStruct((WIDTH, LANES), F3...  59.4 us
    unnamed x24, local copies, waits for them, and re-layouts  7.82 us

profile of v1, /device:TPU:1, one launch (start us, length us, event | category | flops | bytes accessed | tf_op | source)
XLA Modules:
  0.0 69.3 jit_solution(4244283829559901341)
XLA Ops:
  0.6 0.0 copy-start.7
  0.6 0.0 copy-start.4
  0.7 0.0 copy-start.5
  0.7 0.7 %broadcast_in_dim.16.act_ref = s32[1,768]{1,0:T(1,128)S(1)} reshape(s32[768]{0:T(1024)} %param.14) | data formatting | bytes 6144 | tf_op jit(solution)/shard_map/broadcast_in_dim | solution.py:499
  1.4 0.0 copy-start.6
  1.4 0.7 %broadcast_in_dim.17.nact_ref = s32[1,768]{1,0:T(1,128)S(1)} reshape(s32[768]{0:T(1024)} %param.15) | data formatting | bytes 6144 | tf_op jit(solution)/shard_map/broadcast_in_dim | solution.py:500
  2.1 0.0 copy-done.7
  2.1 0.0 copy-done.4
  2.1 0.0 copy-done.5
  2.1 0.0 copy-done.6
  2.1 0.0 copy-start
  2.1 1.0 %copy-done = bf16[256,1024]{1,0:T(8,128)(2,1)S(1)} copy-done((bf16[256,1024]{1,0:T(8,128)(2,1)S(1)}, bf16[256,1024]{1,0:T(8,128)(2,1)}, u32[]{:S(2)}) %copy-start) | copy-done | bytes 524312
  3.1 0.0 copy-start.1
  3.1 1.0 %copy-done.1 = bf16[1,1024,256]{2,1,0:T(8,128)(2,1)S(1)} copy-done((bf16[1,1024,256]{2,1,0:T(8,128)(2,1)S(1)}, bf16[1,1024,256]{2,1,0:T(8,128)(2,1)}, u32[]{:S(2)}) %copy-start.1) | copy-done | bytes 524312
  4.2 0.0 copy-start.2
  4.2 1.0 %copy-done.2 = bf16[1,256,1024]{2,1,0:T(8,128)(2,1)S(1)} copy-done((bf16[1,256,1024]{2,1,0:T(8,128)(2,1)S(1)}, bf16[1,256,1024]{2,1,0:T(8,128)(2,1)}, u32[]{:S(2)}) %copy-start.2) | copy-done | bytes 524312
  5.2 0.0 copy-start.3
  5.2 0.9 %copy-done.3 = bf16[1,1024,128]{2,1,0:T(8,128)(2,1)S(1)} copy-done((bf16[1,1024,128]{2,1,0:T(8,128)(2,1)S(1)}, bf16[1,1024,128]{2,1,0:T(8,128)(2,1)}, u32[]{:S(2)}) %copy-start.3) | copy-done | bytes 262168
  6.2 0.0 copy-start.8
  6.2 0.7 copy-done.8
  6.8 0.0 copy-start.9
  6.8 0.7 copy-done.9
  7.5 59.4 %rollout.1 = (f32[1024,128]{1,0:T(8,128)S(1)}, f32[18,128]{1,0:T(8,128)S(1)}, f32[1,128]{1,0:T(1,128)S(1)}, f32[1,24]{1,0:T(1,128)S(1)}) custom-call(s32[1,24]{1,0:T(1,128)S(1)} %bitcast.16, s32[1,768]{1,0:T(1,128)S(1)} %broadcast_in_dim.16.act_ref, s32[1,768]{1,0:T(1,128)S(1)} %broadcast_in_dim.17.nact_ref, s32[1,768]{1,0:T(1,128)S(1)} %copy-done.7, ...), custom_call_target="tpu_custom_call" | custom-call | tf_op jit(solution)/shard_map/rollout/pallas_call | solution.py:442
  66.9 0.6 copy.16
  67.5 0.8 %copy.20 = f32[1,1024,128]{2,1,0:T(8,128)} copy(f32[1,1024,128]{2,1,0:T(8,128)S(1)} %bitcast.11) | data formatting | bytes 1048576
  68.3 0.5 copy.21
  68.8 0.5 copy.22
Async XLA Ops:
  0.6 1.4 %copy-start.7 = (s32[1,768]{1,0:T(1,128)S(1)}, s32[1,768]{1,0:T(1,128)}, u32[]{:S(2)}) copy-start(s32[1,768]{1,0:T(1,128)} %boot_ref.1) | copy-start | bytes 9220
  0.6 1.4 %copy-start.4 = (bf16[1,18,256]{2,1,0:T(8,128)(2,1)S(1)}, bf16[1,18,256]{2,1,0:T(8,128)(2,1)}, u32[]{:S(2)}) copy-start(bf16[1,18,256]{2,1,0:T(8,128)(2,1)} %param.18) | copy-start | bytes 27652
  0.7 1.4 %copy-start.5 = (bf16[1,18,128]{2,1,0:T(8,128)(2,1)S(1)}, bf16[1,18,128]{2,1,0:T(8,128)(2,1)}, u32[]{:S(2)}) copy-start(bf16[1,18,128]{2,1,0:T(8,128)(2,1)} %param.22) | copy-start | bytes 13828
  1.4 0.7 %copy-start.6 = (bf16[1,1024]{1,0:T(2,128)(2,1)S(1)}, bf16[1,1024]{1,0:T(2,128)(2,1)}, u32[]{:S(2)}) copy-start(bf16[1,1024]{1,0:T(2,128)(2,1)} %rhead_ref.1) | copy-start | bytes 6148
  2.1 1.0 %copy-start = (bf16[256,1024]{1,0:T(8,128)(2,1)S(1)}, bf16[256,1024]{1,0:T(8,128)(2,1)}, u32[]{:S(2)}) copy-start(bf16[256,1024]{1,0:T(8,128)(2,1)} %logged_hbm.1) | copy-start | bytes 1572868
  3.1 1.0 %copy-start.1 = (bf16[1,1024,256]{2,1,0:T(8,128)(2,1)S(1)}, bf16[1,1024,256]{2,1,0:T(8,128)(2,1)}, u32[]{:S(2)}) copy-start(bf16[1,1024,256]{2,1,0:T(8,128)(2,1)} %param.17) | copy-start | bytes 1572868
  4.2 1.0 %copy-start.2 = (bf16[1,256,1024]{2,1,0:T(8,128)(2,1)S(1)}, bf16[1,256,1024]{2,1,0:T(8,128)(2,1)}, u32[]{:S(2)}) copy-start(bf16[1,256,1024]{2,1,0:T(8,128)(2,1)} %param.19) | copy-start | bytes 1572868
  5.2 0.9 %copy-start.3 = (bf16[1,1024,128]{2,1,0:T(8,128)(2,1)S(1)}, bf16[1,1024,128]{2,1,0:T(8,128)(2,1)}, u32[]{:S(2)}) copy-start(bf16[1,1024,128]{2,1,0:T(8,128)(2,1)} %param.21) | copy-start | bytes 786436
  6.2 0.7 copy-start.8
  6.8 0.7 copy-start.9

commit v2 on v1

v2 whole, which is shorter than its diff:
```python
import jax
import jax.numpy as jnp
from jax import lax
from jax.experimental import pallas as pl
from jax.experimental.pallas import tpu as pltpu
from jax.sharding import PartitionSpec as P

MESH = pl.DeviceIdType.MESH
F32 = jnp.float32
BF16 = jnp.bfloat16

discount = 0.99
penalty_weight = 1.0

CHUNKS = 3
CHIPS = 16
SIDE = 4
MEMBERS = 16
WIDTH = 1024
HALF = 512
LANES = 128
ACTS = 32

AG1_GROUP = 1
RS_GROUP = 1
AG2_GROUP = 1

HOPS = (0, 1, 2, 1)
PLANE_ORDER = sorted(
    [(other, step) for other in range(2) for step in range(CHIPS) if other or step],
    key=lambda pair: (-HOPS[pair[1] // SIDE] - HOPS[pair[1] % SIDE], pair),
)
Z_ORDER = (8, 7, 9, 6, 10, 5, 11, 4, 12, 3, 13, 2, 14, 1, 15)


def nt(lhs, rhs):
    return lax.dot_general(lhs, rhs, (((1,), (1,)), ((), ())), preferred_element_type=F32)


def tn(lhs, rhs):
    return lax.dot_general(lhs, rhs, (((0,), (0,)), ((), ())), preferred_element_type=F32)


def nn(lhs, rhs):
    return jnp.dot(lhs, rhs, preferred_element_type=F32)


def sigmoid(v):
    return 0.5 * jnp.tanh(0.5 * v) + 0.5


def fold(block):
    return jnp.concatenate([block[:, :HALF], block[:, HALF:]], axis=0)


def unfold(block):
    return jnp.concatenate([block[:8], block[8:]], axis=1)


def iota(shape, dim):
    return lax.broadcasted_iota(jnp.int32, shape, dim)


def kernel(
    rowid_hbm,
    act_hbm,
    nact_hbm,
    boot_hbm,
    rhead_hbm,
    chead_hbm,
    demb_hbm,
    cemb_hbm,
    logged_hbm,
    din_hbm,
    dout_hbm,
    cin_hbm,
    gin_ref,
    gemb_ref,
    ghead_ref,
    tgt_ref,
    rowid_ref,
    act_ref,
    nact_ref,
    boot_ref,
    rhead_ref,
    chead_ref,
    demb_ref,
    cemb_ref,
    logv,
    wi,
    wo,
    wc,
    em,
    ce,
    hd,
    ag1,
    xs,
    ep,
    rss,
    rsr,
    ag2,
    wct,
    ecn,
    ecb,
    at,
    gt,
    xt,
    bt,
    acts,
    cnt,
    qv,
    ph6,
    zb,
    loc_sem,
    wsend,
    wrecv,
    a_send,
    a_recv,
    r_send,
    r_recv,
    n_send,
    n_recv,
    x_send,
    x_recv,
    s_send,
    s_recv,
):
    dp = lax.axis_index("dp")
    zi = lax.axis_index("mp")
    core = dp % 2
    me = dp // 2
    px = me % SIDE
    py = me // SIDE
    sib = (dp + 1 - 2 * core, zi)

    def peer(step, other=0):
        chip = ((py + step // SIDE) % SIDE) * SIDE + (px + step % SIDE) % SIDE
        return chip, (chip * 2 + (core + other) % 2, zi)

    loads = [
        pltpu.make_async_copy(src, dst, loc_sem.at[i])
        for i, (src, dst) in enumerate(
            [
                (logged_hbm, logv),
                (rowid_hbm, rowid_ref),
                (demb_hbm, demb_ref),
                (cemb_hbm, cemb_ref),
                (chead_hbm, chead_ref),
                (act_hbm, act_ref),
                (nact_hbm, nact_ref),
                (boot_hbm, boot_ref),
                (rhead_hbm, rhead_ref),
                (din_hbm, wi.at[0]),
                (dout_hbm, wo.at[0]),
                (cin_hbm, wc.at[0]),
            ]
        )
    ]
    for load in loads[:2]:
        load.start()

    barrier = pltpu.get_barrier_semaphore()
    for step in Z_ORDER:
        pl.semaphore_signal(barrier, inc=1, device_id=(dp, (zi + step) % MEMBERS), device_id_type=MESH)
    for other, step in PLANE_ORDER:
        pl.semaphore_signal(barrier, inc=1, device_id=peer(step, other)[1], device_id_type=MESH)
    for load in loads[2:]:
        load.start()

    loads[0].wait()
    loads[1].wait()
    hot = (iota((256, 24), 0) == rowid_ref[...].reshape(1, 24)).astype(BF16)
    picked = tn(hot, logv[...])
    for ch in range(CHUNKS):
        ag1[me, ch] = fold(picked[ch * 8 : ch * 8 + 8]).astype(BF16)
    pl.semaphore_wait(barrier, 31 + MEMBERS - 1)

    def spread(src, dst, send_sem, recv_sem, first, count):
        def one(step):
            chip, where = peer(step)
            pltpu.make_async_remote_copy(
                src_ref=src(chip).at[pl.ds(first, count)],
                dst_ref=dst.at[me, pl.ds(first, count)],
                send_sem=send_sem.at[first],
                recv_sem=recv_sem.at[first],
                device_id=where,
                device_id_type=MESH,
            ).start()

        for other, step in PLANE_ORDER:
            if other == 0:
                one(step)

    def landed(buf, sem, first, count):
        slots = buf.at[pl.ds(0, CHIPS - 1), pl.ds(first, count)]
        pltpu.make_async_copy(slots, slots, sem.at[first]).wait()

    for first in range(0, CHUNKS, AG1_GROUP):
        spread(lambda chip: ag1.at[me], ag1, a_send, a_recv, first, AG1_GROUP)

    for load in loads[2:]:
        load.wait()
    eye = (iota((ACTS, 18), 0) == iota((ACTS, 18), 1)).astype(BF16)
    em[0] = nn(eye, demb_ref[...]).astype(BF16)
    ce[0] = nn(eye, cemb_ref[...]).astype(BF16)
    hd[0] = jnp.broadcast_to(chead_ref[...].astype(F32), (8, LANES))

    swaps = []
    for i, (src, dst) in enumerate(
        [
            (din_hbm, wi.at[1]),
            (em.at[0], em.at[1]),
            (dout_hbm, wo.at[1]),
            (cin_hbm, wc.at[1]),
            (ce.at[0], ce.at[1]),
            (hd.at[0], hd.at[1]),
        ]
    ):
        swaps.append(
            pltpu.make_async_remote_copy(
                src_ref=src,
                dst_ref=dst,
                send_sem=wsend.at[i],
                recv_sem=wrecv.at[i],
                device_id=sib,
                device_id_type=MESH,
            )
        )
        swaps[-1].start()

    lane = iota((1, LANES), 1)
    base = 48 * (lane // 8) + lane % 8
    stacked = jnp.concatenate(
        [
            act_ref[...].reshape(1, 768).astype(F32),
            nact_ref[...].reshape(1, 768).astype(F32),
            jnp.zeros((6, 768), F32),
        ],
        axis=0,
    ).astype(BF16)
    columns = [
        jnp.broadcast_to(boot_ref[:, part * LANES : (part + 1) * LANES].astype(F32), (LANES, LANES)).T
        for part in range(6)
    ]
    for half in range(2):
        who = core if half == 0 else 1 - core
        for ch in range(CHUNKS):
            rows = base + 24 * who + 8 * ch
            pick = (iota((768, LANES), 0) == rows).astype(BF16)
            acts[half * CHUNKS + ch] = nn(stacked, pick)
            total = jnp.zeros((LANES, LANES), F32)
            for column in columns:
                total = total + (column == rows.astype(F32)).astype(F32)
            cnt[half * CHUNKS + ch] = jnp.broadcast_to(jnp.sum(total, axis=0, keepdims=True), (8, LANES))

    def hot_t(slot, row):
        return (iota((ACTS, LANES), 0).astype(F32) == acts[slot][row : row + 1]).astype(BF16)

    for ch in range(CHUNKS):
        ep[ch, 0] = tn(hot_t(ch, 0), em[0])
    swaps[0].wait_recv()
    swaps[1].wait_recv()
    for ch in range(CHUNKS):
        ep[ch, 1] = tn(hot_t(ch, 0), em[1])
    swaps[2].wait_recv()

    for ch in range(CHUNKS):
        if ch % AG1_GROUP == 0:
            landed(ag1, a_recv, ch, AG1_GROUP)
        x = jnp.concatenate([unfold(ag1[j, ch].astype(F32)) for j in range(CHIPS)], axis=0).astype(BF16)
        xs[0, ch] = x
        pltpu.make_async_remote_copy(
            src_ref=xs.at[0, ch],
            dst_ref=xs.at[1, ch],
            send_sem=x_send.at[ch],
            recv_sem=x_recv.at[ch],
            device_id=sib,
            device_id_type=MESH,
        ).start()
        inc = jnp.zeros((LANES, WIDTH), F32)
        for s in range(2):
            pre = nn(x, wi[s]) + ep[ch, s]
            inc = inc + nn((pre * sigmoid(pre)).astype(BF16), wo[s])
        for j in range(CHIPS):
            rss[j, ch] = fold(inc[j * 8 : j * 8 + 8]).astype(BF16)
        rsr[me, ch] = rss[me, ch]
        if (ch + 1) % RS_GROUP == 0:
            spread(lambda chip: rss.at[chip], rsr, r_send, r_recv, ch + 1 - RS_GROUP, RS_GROUP)

    for i in range(3, 6):
        swaps[i].wait_recv()
    for s in range(2):
        wct[s * LANES : (s + 1) * LANES] = wc[s].T
    wct[256:272] = jnp.concatenate([rhead_ref[...].astype(F32), jnp.zeros((15, WIDTH), F32)], axis=0).astype(BF16)
    heads = [jnp.broadcast_to(hd[s][:1], (LANES, LANES)).T for s in range(2)]
    for ch in range(CHUNKS):
        for s in range(2):
            ecn[ch, s] = tn(ce[s], hot_t(ch, 1))
            ecb[ch, s] = tn(ce[s], hot_t(ch, 0))
        ecb[CHUNKS + ch, 0] = tn(ce[0], hot_t(CHUNKS + ch, 0))

    def own_units(slot, pre):
        gate = sigmoid(pre)
        act = pre * gate
        at[slot] = act
        gt[slot] = heads[0] * (gate * (1.0 + pre * (1.0 - gate)))
        return act

    for ch in range(CHUNKS):
        x = xs[0, ch]
        pre = nt(wct[:256], x)
        act0 = own_units(ch, pre[:LANES] + ecb[ch, 0])
        pre1 = pre[LANES:] + ecb[ch, 1]
        weighted = act0 * heads[0] + pre1 * sigmoid(pre1) * heads[1]
        qv[ch : ch + 1] = jnp.sum(weighted, axis=0, keepdims=True)
        xt[:, ch * LANES : (ch + 1) * LANES] = x.T

    for swap in swaps:
        swap.wait_send()
    for first in range(0, CHUNKS, AG1_GROUP):
        landed(ag1, a_send, first, AG1_GROUP)

    for ch in range(CHUNKS):
        if ch % RS_GROUP == 0:
            landed(rsr, r_recv, ch, RS_GROUP)
        total = rsr[0, ch].astype(F32)
        for j in range(1, CHIPS):
            total = total + rsr[j, ch].astype(F32)
        ag2[me, ch] = (ag1[me, ch].astype(F32) + total).astype(BF16)
        if (ch + 1) % AG2_GROUP == 0:
            spread(lambda chip: ag2.at[me], ag2, n_send, n_recv, ch + 1 - AG2_GROUP, AG2_GROUP)

    for ch in range(CHUNKS):
        pltpu.make_async_copy(xs.at[1, ch], xs.at[1, ch], x_recv.at[ch]).wait()
        x = xs[1, ch]
        own_units(CHUNKS + ch, nt(wct[:LANES], x) + ecb[CHUNKS + ch, 0])
        xt[:, (CHUNKS + ch) * LANES : (CHUNKS + ch + 1) * LANES] = x.T

    for ch in range(CHUNKS):
        pltpu.make_async_copy(xs.at[0, ch], xs.at[0, ch], x_send.at[ch]).wait()
    for first in range(0, CHUNKS, RS_GROUP):
        landed(rss, r_send, first, RS_GROUP)

    for ch in range(CHUNKS):
        if ch % AG2_GROUP == 0:
            landed(ag2, n_recv, ch, AG2_GROUP)
        x = jnp.concatenate([unfold(ag2[j, ch].astype(F32)) for j in range(CHIPS)], axis=0).astype(BF16)
        pre = nt(wct[...], x)
        pre0 = pre[:LANES] + ecn[ch, 0]
        pre1 = pre[LANES:256] + ecn[ch, 1]
        weighted = pre0 * sigmoid(pre0) * heads[0] + pre1 * sigmoid(pre1) * heads[1]
        value = jnp.sum(weighted, axis=0, keepdims=True)
        ph6[me, ch : ch + 1] = discount * value + jnp.where(lane // 8 == me, pre[256:257], 0.0)
    ph6[me, 3:6] = qv[0:3]

    def share(other, step):
        return pltpu.make_async_remote_copy(
            src_ref=ph6.at[me],
            dst_ref=ph6.at[other * CHIPS + me],
            send_sem=s_send.at[0],
            recv_sem=s_recv.at[0],
            device_id=peer(step, other)[1],
            device_id_type=MESH,
        )

    for other, step in PLANE_ORDER:
        share(other, step).start()
    for first in range(0, CHUNKS, AG2_GROUP):
        landed(ag2, n_send, first, AG2_GROUP)
    slots = ph6.at[pl.ds(0, 31)]
    pltpu.make_async_copy(slots, slots, s_recv.at[0]).wait()
    halves = []
    for half in range(2):
        sums = ph6[half * CHIPS]
        for j in range(1, CHIPS):
            sums = sums + ph6[half * CHIPS + j]
        halves.append(sums)
    zb[zi] = jnp.concatenate([halves[0][:3], halves[1][:3], jnp.zeros((2, LANES), F32)], axis=0)
    for step in Z_ORDER:
        pltpu.make_async_remote_copy(
            src_ref=zb.at[zi],
            dst_ref=zb.at[zi],
            send_sem=s_send.at[1],
            recv_sem=s_recv.at[1],
            device_id=(dp, (zi + step) % MEMBERS),
            device_id_type=MESH,
        ).start()
    slots = ph6.at[pl.ds(0, 31)]
    pltpu.make_async_copy(slots, slots, s_send.at[0]).wait()
    slots = zb.at[pl.ds(0, MEMBERS - 1)]
    pltpu.make_async_copy(slots, slots, s_recv.at[1]).wait()
    total = zb[0]
    square = total * total
    for m in range(1, MEMBERS):
        one = zb[m]
        total = total + one
        square = square + one * one
    mean = total / MEMBERS
    spread = square / MEMBERS - mean * mean
    target = mean - penalty_weight * jnp.sqrt(spread + 1.0)

    turned = pltpu.roll(target, (LANES - 8 * me) % LANES, 1)
    line = turned[0:1]
    for ch in range(1, CHUNKS):
        line = jnp.where(lane // 8 == ch, pltpu.roll(turned, 8 * ch, 1)[ch : ch + 1], line)
    tgt_ref[...] = line[:, :24]

    head_sum = jnp.zeros((LANES, LANES), F32)
    for half in range(2):
        for ch in range(CHUNKS):
            slot = half * CHUNKS + ch
            scaled = cnt[slot][:1] * (halves[half][3 + ch : 4 + ch] - target[slot : slot + 1])
            head_sum = head_sum + scaled * at[slot]
            bt[:, slot * LANES : (slot + 1) * LANES] = (scaled * gt[slot]).astype(BF16)
    back = bt[...]
    gin_ref[...] = nt(xt[...], back)
    hots = jnp.concatenate([hot_t(slot, 0) for slot in range(2 * CHUNKS)], axis=1)
    gemb_ref[...] = nt(hots, back)[:18].reshape(18, 1, LANES)
    ghead_ref[...] = jnp.sum(head_sum.T, axis=0, keepdims=True)

    slots = zb.at[pl.ds(0, MEMBERS - 1)]
    pltpu.make_async_copy(slots, slots, s_send.at[1]).wait()


def finish(gin_ref, gemb_ref, ghead_ref, tgt_ref, gin_out, gemb_out, ghead_out, tgt_out, sem):
    copies = [
        pltpu.make_async_copy(src, dst, sem.at[i])
        for i, (src, dst) in enumerate(
            [(gin_ref, gin_out), (gemb_ref, gemb_out), (ghead_ref, ghead_out), (tgt_ref, tgt_out)]
        )
    ]
    for copy in copies:
        copy.start()
    for copy in copies:
        copy.wait()


def local(
    logged,
    row_ids,
    actions,
    next_actions,
    boot,
    dyn_in,
    dyn_embed,
    dyn_out,
    reward_head,
    critic_in,
    critic_embed,
    critic_head,
):
    vmem = pl.BlockSpec(memory_space=pltpu.VMEM)
    hbm = pl.BlockSpec(memory_space=pltpu.HBM)
    dma = pltpu.SemaphoreType.DMA
    blocks = (CHIPS, CHUNKS, 16, HALF)
    shapes = (
        jax.ShapeDtypeStruct((WIDTH, LANES), F32),
        jax.ShapeDtypeStruct((18, 1, LANES), F32),
        jax.ShapeDtypeStruct((1, LANES), F32),
        jax.ShapeDtypeStruct((1, 24), F32),
    )
    results = pl.pallas_call(
        kernel,
        out_shape=shapes,
        in_specs=[hbm] * 12,
        out_specs=(vmem,) * 4,
        scratch_shapes=[
            pltpu.VMEM((24,), jnp.int32),
            pltpu.VMEM((768,), jnp.int32),
            pltpu.VMEM((768,), jnp.int32),
            pltpu.VMEM((1, 768), jnp.int32),
            pltpu.VMEM((1, WIDTH), BF16),
            pltpu.VMEM((1, LANES), BF16),
            pltpu.VMEM((18, 256), BF16),
            pltpu.VMEM((18, LANES), BF16),
            pltpu.VMEM((256, WIDTH), BF16),
            pltpu.VMEM((2, WIDTH, 256), BF16),
            pltpu.VMEM((2, 256, WIDTH), BF16),
            pltpu.VMEM((2, WIDTH, LANES), BF16),
            pltpu.VMEM((2, ACTS, 256), BF16),
            pltpu.VMEM((2, ACTS, LANES), BF16),
            pltpu.VMEM((2, 8, LANES), F32),
            pltpu.VMEM(blocks, BF16),
            pltpu.VMEM((2, CHUNKS, LANES, WIDTH), BF16),
            pltpu.VMEM((CHUNKS, 2, LANES, 256), F32),
            pltpu.VMEM(blocks, BF16),
            pltpu.VMEM(blocks, BF16),
            pltpu.VMEM(blocks, BF16),
            pltpu.VMEM((272, WIDTH), BF16),
            pltpu.VMEM((CHUNKS, 2, LANES, LANES), F32),
            pltpu.VMEM((2 * CHUNKS, 2, LANES, LANES), F32),
            pltpu.VMEM((2 * CHUNKS, LANES, LANES), F32),
            pltpu.VMEM((2 * CHUNKS, LANES, LANES), F32),
            pltpu.VMEM((WIDTH, 768), BF16),
            pltpu.VMEM((LANES, 768), BF16),
            pltpu.VMEM((2 * CHUNKS, 8, LANES), F32),
            pltpu.VMEM((2 * CHUNKS, 8, LANES), F32),
            pltpu.VMEM((8, LANES), F32),
            pltpu.VMEM((2 * CHIPS, 8, LANES), F32),
            pltpu.VMEM((MEMBERS, 8, LANES), F32),
            dma((12,)),
            dma((6,)),
            dma((6,)),
            dma((CHUNKS,)),
            dma((CHUNKS,)),
            dma((CHUNKS,)),
            dma((CHUNKS,)),
            dma((CHUNKS,)),
            dma((CHUNKS,)),
            dma((CHUNKS,)),
            dma((CHUNKS,)),
            dma((2,)),
            dma((2,)),
        ],
        compiler_params=pltpu.CompilerParams(
            collective_id=0, has_side_effects=True, vmem_limit_bytes=60 * 2**20
        ),
        name="rollout",
    )(
        row_ids,
        actions,
        next_actions,
        boot,
        reward_head,
        critic_head,
        dyn_embed[0],
        critic_embed[0],
        logged,
        dyn_in[0],
        dyn_out[0],
        critic_in[0],
    )
    grad_in, grad_embed, grad_head, target = pl.pallas_call(
        finish,
        out_shape=shapes,
        in_specs=[vmem] * 4,
        out_specs=(hbm,) * 4,
        scratch_shapes=[dma((4,))],
        compiler_params=pltpu.CompilerParams(vmem_limit_bytes=60 * 2**20),
        name="finish",
    )(*results)
    return grad_in[None], grad_embed.transpose(1, 0, 2), grad_head, target[0]


def solution(mesh):
    return jax.shard_map(
        local,
        mesh=mesh,
        in_specs=(
            P("dp", None),
            P("dp"),
            P(),
            P(),
            P("mp", None),
            P("mp", None, "dp"),
            P("mp", None, "dp"),
            P("mp", "dp", None),
            P("mp", None),
            P("mp", None, "dp"),
            P("mp", None, "dp"),
            P("mp", "dp"),
        ),
        out_specs=(P("mp", None, "dp"), P("mp", None, "dp"), P("mp", "dp"), P("dp")),
        check_vma=False,
    )
```

time: 69.7 us -> 60.6 us (0.87)
  local copies, waits for them, and re-layouts: 9.23 us -> 0 us
    unnamed x24 -> x0, local copies, waits for them, and re-layouts: 7.82 us -> none
    broadcast_in_dim x2 -> x0, local copies, waits for them, and re-layouts: 1.41 us -> none  [the longest x1 0.71 us: local(): actions[None]]
    pallas_call x1 -> x2, Pallas kernels: 59.4 us -> 59.8 us  [the longest x1 57.9 us: local(): pl.pallas_call(kernel, out_shape=shapes, in_specs=[hbm] * 12, out_specs=(...]
where the time goes in v2:
time: 60.6 us; the launch traced here: 60.4 us
  Pallas kernels  59.8 us (99%)
  between operations  0.64 us (1%)
    pallas_call x1, Pallas kernels, local(): pl.pallas_call(kernel, out_shape=shapes, in_specs=[hbm] * 12, out_specs=(...  57.9 us
    pallas_call x1, Pallas kernels, local(): pl.pallas_call(finish, out_shape=shapes, in_specs=[vmem] * 4, out_specs=(...  1.9 us

profile of v2, /device:TPU:1, one launch (start us, length us, event | category | flops | bytes accessed | tf_op | source)
XLA Modules:
  0.0 60.4 jit_solution(83953142574758875)
XLA Ops:
  0.6 57.9 %rollout.1 = (f32[1024,128]{1,0:T(8,128)}, f32[18,1,128]{2,1,0:T(1,128)}, f32[1,128]{1,0:T(1,128)}, f32[1,24]{1,0:T(1,128)}) custom-call(s32[24]{0:T(128)} %rowid_hbm.1, s32[768]{0:T(1024)} %act_hbm.1, s32[768]{0:T(1024)} %nact_hbm.1, s32[1,768]{1,0:T(1,128)} %boot_hbm.1, bf16[1,1024]{1,0:T(2,128)(2,1)} %rhead_hbm.1, bf16[1,128]{1,0:T(2,128)(2,1)} %chead_hbm.1, ...), custom_call_target="tpu_custom_call" | custom-call | tf_op jit(solution)/shard_map/rollout/pallas_call | solution.py:462
  58.5 1.9 %finish.1 = (f32[1024,128]{1,0:T(8,128)}, f32[18,1,128]{2,1,0:T(1,128)}, f32[1,128]{1,0:T(1,128)}, f32[1,24]{1,0:T(1,128)}) custom-call(f32[1024,128]{1,0:T(8,128)} %get-tuple-element.12.gin_ref, f32[18,1,128]{2,1,0:T(1,128)} %get-tuple-element.13.gemb_ref, f32[1,128]{1,0:T(1,128)} %get-tuple-element.14.ghead_ref, f32[1,24]{1,0:T(1,128)} %get-tuple-element.15.tgt_ref), custom_call_target="tpu_custom_call" | custom-call | tf_op jit(solution)/shard_map/finish/pallas_call | solution.py:533

commit v3 on v2

--- a/solution.py
+++ b/solution.py
@@ -169,7 +169,7 @@
 
     loads[0].wait()
     loads[1].wait()
-    hot = (iota((256, 24), 0) == rowid_ref[...].reshape(1, 24)).astype(BF16)
+    hot = (iota((256, 24), 0) == rowid_ref[...]).astype(BF16)
     picked = tn(hot, logv[...])
     for ch in range(CHUNKS):
         ag1[me, ch] = fold(picked[ch * 8 : ch * 8 + 8]).astype(BF16)
@@ -415,7 +415,7 @@
     back = bt[...]
     gin_ref[...] = nt(xt[...], back)
     hots = jnp.concatenate([hot_t(slot, 0) for slot in range(2 * CHUNKS)], axis=1)
-    gemb_ref[...] = nt(hots, back)[:18].reshape(18, 1, LANES)
+    gemb_ref[...] = nt(hots, back).reshape(ACTS, 1, LANES)
     ghead_ref[...] = jnp.sum(head_sum.T, axis=0, keepdims=True)
 
     slots = zb.at[pl.ds(0, MEMBERS - 1)]
@@ -426,7 +426,7 @@
     copies = [
         pltpu.make_async_copy(src, dst, sem.at[i])
         for i, (src, dst) in enumerate(
-            [(gin_ref, gin_out), (gemb_ref, gemb_out), (ghead_ref, ghead_out), (tgt_ref, tgt_out)]
+            [(gin_ref, gin_out), (gemb_ref.at[pl.ds(0, 18)], gemb_out), (ghead_ref, ghead_out), (tgt_ref, tgt_out)]
         )
     ]
     for copy in copies:
@@ -453,19 +453,18 @@
     hbm = pl.BlockSpec(memory_space=pltpu.HBM)
     dma = pltpu.SemaphoreType.DMA
     blocks = (CHIPS, CHUNKS, 16, HALF)
-    shapes = (
-        jax.ShapeDtypeStruct((WIDTH, LANES), F32),
-        jax.ShapeDtypeStruct((18, 1, LANES), F32),
-        jax.ShapeDtypeStruct((1, LANES), F32),
-        jax.ShapeDtypeStruct((1, 24), F32),
-    )
+    def shapes(rows):
+        return tuple(
+            jax.ShapeDtypeStruct(shape, F32) for shape in ((WIDTH, LANES), (rows, 1, LANES), (1, LANES), (1, 24))
+        )
+
     results = pl.pallas_call(
         kernel,
-        out_shape=shapes,
+        out_shape=shapes(ACTS),
         in_specs=[hbm] * 12,
         out_specs=(vmem,) * 4,
         scratch_shapes=[
-            pltpu.VMEM((24,), jnp.int32),
+            pltpu.VMEM((1, 24), jnp.int32),
             pltpu.VMEM((768,), jnp.int32),
             pltpu.VMEM((768,), jnp.int32),
             pltpu.VMEM((1, 768), jnp.int32),
@@ -517,7 +516,7 @@
         ),
         name="rollout",
     )(
-        row_ids,
+        row_ids[None],
         actions,
         next_actions,
         boot,
@@ -532,7 +531,7 @@
     )
     grad_in, grad_embed, grad_head, target = pl.pallas_call(
         finish,
-        out_shape=shapes,
+        out_shape=shapes(18),
         in_specs=[vmem] * 4,
         out_specs=(hbm,) * 4,
         scratch_shapes=[dma((4,))],

time: 60.6 us -> 60.6 us (level)
  no operation moved by 1% of the time
where the time goes in v3:
time: 60.6 us; the launch traced here: 60.4 us
  Pallas kernels  59.8 us (99%)
  between operations  0.64 us (1%)
    pallas_call x1, Pallas kernels, local(): pl.pallas_call(kernel, out_shape=shapes(ACTS), in_specs=[hbm] * 12, out_s...  57.9 us
    pallas_call x1, Pallas kernels, local(): pl.pallas_call(finish, out_shape=shapes(18), in_specs=[vmem] * 4, out_spe...  1.9 us

profile of v3, /device:TPU:1, one launch (start us, length us, event | category | flops | bytes accessed | tf_op | source)
XLA Modules:
  0.0 60.4 jit_solution(14406392214122045598)
XLA Ops:
  0.6 57.9 %rollout.1 = (f32[1024,128]{1,0:T(8,128)}, f32[32,1,128]{2,1,0:T(1,128)}, f32[1,128]{1,0:T(1,128)}, f32[1,24]{1,0:T(1,128)}) custom-call(s32[1,24]{1,0:T(1,128)} %bitcast.14, s32[768]{0:T(1024)} %act_hbm.1, s32[768]{0:T(1024)} %nact_hbm.1, s32[1,768]{1,0:T(1,128)} %boot_hbm.1, bf16[1,1024]{1,0:T(2,128)(2,1)} %rhead_hbm.1, bf16[1,128]{1,0:T(2,128)(2,1)} %chead_hbm.1, ...), custom_call_target="tpu_custom_call" | custom-call | tf_op jit(solution)/shard_map/rollout/pallas_call | solution.py:461
  58.5 1.9 %finish.1 = (f32[1024,128]{1,0:T(8,128)}, f32[18,1,128]{2,1,0:T(1,128)}, f32[1,128]{1,0:T(1,128)}, f32[1,24]{1,0:T(1,128)}) custom-call(f32[1024,128]{1,0:T(8,128)} %get-tuple-element.12.gin_ref, f32[32,1,128]{2,1,0:T(1,128)} %get-tuple-element.13.gemb_ref, f32[1,128]{1,0:T(1,128)} %get-tuple-element.14.ghead_ref, f32[1,24]{1,0:T(1,128)} %get-tuple-element.15.tgt_ref), custom_call_target="tpu_custom_call" | custom-call | tf_op jit(solution)/shard_map/finish/pallas_call | solution.py:532

commit v4 on v3

--- a/solution.py
+++ b/solution.py
@@ -133,9 +133,14 @@
     py = me // SIDE
     sib = (dp + 1 - 2 * core, zi)
 
+    down = [(py + k) % SIDE * SIDE for k in range(SIDE)]
+    across = [(px + k) % SIDE for k in range(SIDE)]
+    cores = (core, 1 - core)
+    along = [(zi + k) % MEMBERS for k in range(MEMBERS)]
+
     def peer(step, other=0):
-        chip = ((py + step // SIDE) % SIDE) * SIDE + (px + step % SIDE) % SIDE
-        return chip, (chip * 2 + (core + other) % 2, zi)
+        chip = down[step // SIDE] + across[step % SIDE]
+        return chip, (2 * chip + cores[other], zi)
 
     loads = [
         pltpu.make_async_copy(src, dst, loc_sem.at[i])
@@ -161,7 +166,7 @@
 
     barrier = pltpu.get_barrier_semaphore()
     for step in Z_ORDER:
-        pl.semaphore_signal(barrier, inc=1, device_id=(dp, (zi + step) % MEMBERS), device_id_type=MESH)
+        pl.semaphore_signal(barrier, inc=1, device_id=(dp, along[step]), device_id_type=MESH)
     for other, step in PLANE_ORDER:
         pl.semaphore_signal(barrier, inc=1, device_id=peer(step, other)[1], device_id_type=MESH)
     for load in loads[2:]:
@@ -382,7 +387,7 @@
             dst_ref=zb.at[zi],
             send_sem=s_send.at[1],
             recv_sem=s_recv.at[1],
-            device_id=(dp, (zi + step) % MEMBERS),
+            device_id=(dp, along[step]),
             device_id_type=MESH,
         ).start()
     slots = ph6.at[pl.ds(0, 31)]

time: 60.6 us -> 60.6 us (level)
  no operation moved by 1% of the time
where the time goes in v4:
time: 60.6 us; the launch traced here: 60.4 us
  Pallas kernels  59.8 us (99%)
  between operations  0.64 us (1%)
    pallas_call x1, Pallas kernels, local(): pl.pallas_call(kernel, out_shape=shapes(ACTS), in_specs=[hbm] * 12, out_s...  57.9 us
    pallas_call x1, Pallas kernels, local(): pl.pallas_call(finish, out_shape=shapes(18), in_specs=[vmem] * 4, out_spe...  1.9 us

profile of v4, /device:TPU:1, one launch (start us, length us, event | category | flops | bytes accessed | tf_op | source)
XLA Modules:
  0.0 60.4 jit_solution(7444909545196715085)
XLA Ops:
  0.6 57.9 %rollout.1 = (f32[1024,128]{1,0:T(8,128)}, f32[32,1,128]{2,1,0:T(1,128)}, f32[1,128]{1,0:T(1,128)}, f32[1,24]{1,0:T(1,128)}) custom-call(s32[1,24]{1,0:T(1,128)} %bitcast.14, s32[768]{0:T(1024)} %act_hbm.1, s32[768]{0:T(1024)} %nact_hbm.1, s32[1,768]{1,0:T(1,128)} %boot_hbm.1, bf16[1,1024]{1,0:T(2,128)(2,1)} %rhead_hbm.1, bf16[1,128]{1,0:T(2,128)(2,1)} %chead_hbm.1, ...), custom_call_target="tpu_custom_call" | custom-call | tf_op jit(solution)/shard_map/rollout/pallas_call | solution.py:466
  58.5 1.9 %finish.1 = (f32[1024,128]{1,0:T(8,128)}, f32[18,1,128]{2,1,0:T(1,128)}, f32[1,128]{1,0:T(1,128)}, f32[1,24]{1,0:T(1,128)}) custom-call(f32[1024,128]{1,0:T(8,128)} %get-tuple-element.12.gin_ref, f32[32,1,128]{2,1,0:T(1,128)} %get-tuple-element.13.gemb_ref, f32[1,128]{1,0:T(1,128)} %get-tuple-element.14.ghead_ref, f32[1,24]{1,0:T(1,128)} %get-tuple-element.15.tgt_ref), custom_call_target="tpu_custom_call" | custom-call | tf_op jit(solution)/shard_map/finish/pallas_call | solution.py:537
